TPU v7x, 128 devices: a whole 4x4x4 slice. The times are simulated.
128 devices in a mesh: wide: 16 (over x, z), narrow: 8 (over y, core).
Axes of the slice: x: 4, y: 4, z: 4, core: 2. Of those that a mesh axis runs over, the one named last changes fastest.
Arguments:
- disp: bfloat16 [4096, 48, 256], P(('wide', 'narrow')), may hold values from -6 to 6
- loads: bfloat16 [4096, 48, 256], P(('wide', 'narrow')), may hold values from -6 to 6
- tiles: bfloat16 [16384, 256, 256], P(('wide', 'narrow')), may hold values from -0.375 to 0.375
- pair_fpatch: int32 [16384], P(('wide', 'narrow')), may hold values from 0 to 31
- pair_sdev: int32 [16384, 1], P(('wide', 'narrow')), may hold values from 0 to 127; in each aligned block of 128 rows (0 to 127, 128 to 255, ...) at most 2 rows name the same one
- pair_spatch: int32 [16384], P(('wide', 'narrow')), may hold values from 0 to 31
Outputs:
- face_disp: float32 [4096, 48, 256], P(('wide', 'narrow'))
- struct_loads: float32 [4096, 48, 256], P(('wide', 'narrow'))
Inputs may be any that keep to these rules, and one draw needn't show every extreme that they name: `pair_sdev`: among the pairs of one device, at most 2 name the same structure device, and some device reaches 2.
All inputs are finite; a program needn't handle non-finite values.
Results may differ from a plain program's by a relative error of at most 0.0003.
Values may be sent and summed in bfloat16 or wider, within the bound.
No kernel may reach another device: no remote copies, remote signals or barrier semaphores. Data moves between devices by JAX's collectives and lax.ppermute only.
A program may use at most 192 MiB of HBM per device.

v0:
```python
import functools

import jax
import jax.numpy as jnp
from jax import lax
from jax.experimental import pallas as pl
from jax.experimental.pallas import tpu as pltpu
from jax.sharding import PartitionSpec as P

ROOM = 12
META = 16
SHIFT = 4
GROUP = 16
STEPS = 128.0
TOP = 32760.0
LIMIT = 63 << 20


def long_way(disp, loads, tiles, pair_fpatch, pair_sdev, pair_spatch):
    n_wide = lax.axis_size("wide")
    n_narrow = lax.axis_size("narrow")
    n_dev = n_wide * n_narrow
    pair_count = tiles.shape[0]
    capacity = max(2, 2 * pair_count // n_dev)
    slot_count = n_dev * capacity
    columns = disp.shape[1]
    node_count = disp.shape[2]
    face_count = loads.shape[2]
    target = pair_sdev
    same_target = target[:, None] == target[None, :]
    earlier = lax.broadcasted_iota(jnp.int32, (pair_count, pair_count), 0) > lax.broadcasted_iota(
        jnp.int32, (pair_count, pair_count), 1
    )
    place = jnp.sum((same_target & earlier).astype(jnp.int32), axis=1)
    slot_of_pair = target * capacity + place
    hits = slot_of_pair[None, :] == jnp.arange(slot_count, dtype=jnp.int32)[:, None]
    filled = jnp.any(hits, axis=1)
    pair_of_slot = jnp.sum(
        jnp.where(hits, jnp.arange(pair_count, dtype=jnp.int32)[None, :], 0), axis=1
    )
    request = jnp.where(filled, pair_spatch[pair_of_slot], -1).reshape(n_dev, capacity)
    asked = lax.all_to_all(request, ("wide", "narrow"), split_axis=0, concat_axis=0, tiled=True)
    wanted = asked >= 0
    picked = disp[jnp.maximum(asked, 0)]
    answer = jnp.where(wanted[:, :, None, None], picked, jnp.zeros_like(picked))
    arrived = lax.all_to_all(answer, ("wide", "narrow"), split_axis=0, concat_axis=0, tiled=True)
    arrived = arrived.reshape(slot_count, columns, node_count)
    moved = arrived[slot_of_pair]
    face_part = jnp.einsum("pcn,pfn->pcf", moved, tiles, preferred_element_type=jnp.float32)
    fluid_onehot = (
        pair_fpatch[None, :] == jnp.arange(loads.shape[0], dtype=jnp.int32)[:, None]
    ).astype(jnp.float32)
    face_disp = jnp.dot(
        fluid_onehot,
        face_part.reshape(pair_count, -1),
        precision=lax.Precision.HIGHEST,
        preferred_element_type=jnp.float32,
    ).reshape(loads.shape[0], columns, face_count)
    pulled = loads[pair_fpatch]
    load_part = jnp.einsum("pcf,pfn->pcn", pulled, tiles, preferred_element_type=jnp.float32)
    outgoing = jnp.where(filled[:, None, None], load_part[pair_of_slot], 0.0).reshape(
        n_dev, capacity, columns, node_count
    )
    returned = lax.all_to_all(outgoing, ("wide", "narrow"), split_axis=0, concat_axis=0, tiled=True)
    returned = returned.reshape(slot_count, columns * node_count)
    struct_onehot = (
        asked.reshape(-1)[None, :] == jnp.arange(disp.shape[0], dtype=jnp.int32)[:, None]
    ).astype(jnp.float32)
    struct_loads = jnp.dot(
        struct_onehot, returned, precision=lax.Precision.HIGHEST, preferred_element_type=jnp.float32
    ).reshape(disp.shape[0], columns, node_count)
    return (face_disp, struct_loads)


def stream(groups, arrive, first, second):
    arrive(0)
    first(0)

    def step(g, carry):
        arrive(g)
        first(g)
        second(g - 1)
        return carry

    lax.fori_loop(1, groups, step, 0)
    second(groups - 1)


def send_kernel(
    n_narrow, fpatch, sdev, spatch, loads, tiles, disp, out, slot, aug,
    buf, parts, most, power, whole, meta, ends, own, count, sems, side, leaving,
):
    n_wide, patches, columns = out.shape[0], disp.shape[0], disp.shape[1]
    groups = tiles.shape[0] // GROUP
    groups = tiles.shape[0] // GROUP

    def tile_copy(g):
        part = pl.ds(g * GROUP, GROUP)
        return pltpu.make_async_copy(tiles.at[part], buf.at[part], sems.at[g])

    for g in range(groups):
        tile_copy(g).start()
    keep = pltpu.make_async_copy(disp, own.at[pl.ds(0, patches)], side.at[0])
    keep.start()
    meta[...] = jnp.zeros_like(meta)
    for w in range(n_wide):
        count[w] = 0
        meta[w, ROOM : ROOM + 1, :] = jnp.full((1, meta.shape[2]), -1, jnp.int32)
    lane = lax.broadcasted_iota(jnp.int32, (1, meta.shape[2]), 1)

    def first(g):
        at = lax.rem(g, 2)
        for i in range(GROUP):
            p = g * GROUP + i
            part = jnp.dot(loads[fpatch[p]], buf[p], preferred_element_type=jnp.float32)
            parts[at, i] = part
            most[at, i : i + 1, :] = jnp.max(jnp.abs(part), axis=0, keepdims=True)

    def second(g):
        at = lax.rem(g, 2)
        steps = jnp.ceil(jnp.log2(jnp.maximum(most[at], 1e-33)) * STEPS)
        unit = TOP * jnp.exp2(steps * (-1.0 / STEPS))
        power[...] = steps.astype(jnp.int32)
        for i in range(GROUP):
            p = g * GROUP + i
            target = sdev[p]
            w = lax.div(target, n_narrow)
            asked = lax.rem(target, n_narrow) * patches + spatch[p]
            seen = count[w]
            count[w] = seen + 1
            place = jnp.minimum(seen, ROOM - 1)
            slot[p] = (w << SHIFT) | place
            rounded = jnp.round(parts[at, i] * unit[i : i + 1, :]).astype(jnp.int32)
            whole[p] = rounded.astype(jnp.int16)
            pltpu.make_async_copy(
                whole.at[p], out.at[w, pl.ds(pl.multiple_of(place * columns, 16), columns)], leaving
            ).start()
            meta[w, pl.ds(place, 1), :] = power[i : i + 1, :]
            names = meta[w, ROOM : ROOM + 1, :]
            meta[w, ROOM : ROOM + 1, :] = jnp.where(lane == place, asked, names)

    stream(groups, lambda g: tile_copy(g).wait(), first, second)
    ends[...] = meta[...].astype(jnp.int16)
    tail = pltpu.make_async_copy(ends, out.at[:, pl.ds(ROOM * columns, META)], side.at[1])
    tail.start()
    fullest = count[0]
    for w in range(1, n_wide):
        fullest = jnp.maximum(fullest, count[w])
    own[patches] = jnp.full(own.shape[1:], fullest.astype(jnp.float32), jnp.float32).astype(own.dtype)
    keep.wait()
    mark = pltpu.make_async_copy(own, aug, side.at[2])
    mark.start()
    pltpu.make_async_copy(whole, whole, leaving).wait()
    tail.wait()
    mark.wait()


def pick_kernel(n_narrow, arrived, table, answer, names, held, gone, meta, wide_names, coming, outs, side):
    n_wide, columns = arrived.shape[0], table.shape[1]
    stride = table.shape[0] // n_narrow
    patches = stride - 1
    ends = pltpu.make_async_copy(arrived.at[:, pl.ds(ROOM * columns, META)], meta, side)
    ends.start()
    loading = [
        pltpu.make_async_copy(
            table.at[pl.ds(b * stride, stride)], held.at[pl.ds(b * stride, stride)], coming.at[b]
        )
        for b in range(n_narrow)
    ]
    for each in loading:
        each.start()
    ends.wait()
    wide_names[...] = meta[...].astype(jnp.int32)[:, ROOM, : wide_names.shape[1]]
    naming = pltpu.make_async_copy(wide_names, names, side)
    naming.start()
    for each in loading:
        each.wait()
    fullest = held[patches, 0:META, :].astype(jnp.float32)
    for b in range(1, n_narrow):
        fullest = jnp.maximum(fullest, held[b * stride + patches, 0:META, :].astype(jnp.float32))
    gone[:, ROOM * columns :, :] = jnp.broadcast_to(fullest, (n_wide,) + fullest.shape).astype(gone.dtype)
    naming.wait()

    def leave(w):
        return pltpu.make_async_copy(gone.at[w], answer.at[w], outs.at[w])

    def send(w, carry):
        for j in range(ROOM):
            name = jnp.maximum(names[w, j], 0)
            gone[w, j * columns : (j + 1) * columns, :] = held[name + lax.div(name, patches)]
        leave(w).start()
        return carry

    lax.fori_loop(0, n_wide, send, 0)
    for w in range(n_wide):
        leave(w).wait()


def total_kernel(n_narrow, names, arrived, total, came, acc, scale, lists, count, coming, outs):
    n_wide, columns = arrived.shape[0], total.shape[1]
    patches = total.shape[0] // n_narrow
    quarter = n_wide // 4
    loading = [
        pltpu.make_async_copy(
            arrived.at[pl.ds(i * quarter, quarter)], came.at[pl.ds(i * quarter, quarter)], coming.at[i]
        )
        for i in range(4)
    ]
    for each in loading:
        each.start()
    for b in range(n_narrow + 1):
        count[b] = 0

    def file(w, carry):
        for j in range(ROOM):
            name = names[w, j]
            held = jnp.maximum(name, 0)
            b = lax.div(held, patches)
            chosen = jnp.where(name >= 0, b, n_narrow)
            k = count[chosen]
            count[chosen] = k + 1
            lists[chosen, k] = (w << 16) | (j << 12) | (j << 8) | (held - b * patches)
        return carry

    lax.fori_loop(0, n_wide, file, 0)
    for b in range(n_narrow):
        lists[b, count[b]] = (META - 1) << 8
    acc[...] = jnp.zeros_like(acc)
    for each in loading:
        each.wait()
    scale[...] = jnp.exp2(came[:, ROOM * columns :, :].astype(jnp.int32).astype(jnp.float32) * (1.0 / STEPS)) * (1.0 / TOP)
    scale[0, META - 1 : META, :] = jnp.zeros((1, scale.shape[2]), jnp.float32)

    def leave(b):
        return pltpu.make_async_copy(acc.at[b % 4], total.at[pl.ds(b * patches, patches)], outs.at[b % 4])

    for b in range(n_narrow):
        at = b % 4
        if b >= 4:
            leave(b - 4).wait()
            acc[at] = jnp.zeros(acc.shape[1:], jnp.float32)

        def add(k, carry):
            terms = []
            for i in range(2):
                entry = lists[b, 2 * k + i]
                patch = entry & 255
                row = (entry >> 8) & 15
                place = (entry >> 12) & 15
                w = entry >> 16
                value = came[w, pl.ds(pl.multiple_of(place * columns, 16), columns), :].astype(jnp.int32).astype(jnp.float32)
                terms.append((patch, value * scale[w, pl.ds(row, 1), :]))
            for patch, term in terms:
                acc[at, patch] += term
            return carry

        lax.fori_loop(0, lax.div(count[b] + 1, 2), add, 0)
        leave(b).start()
    for b in range(n_narrow - 4, n_narrow):
        leave(b).wait()


def face_kernel(fpatch, slot, arrived, tiles, face, over, buf, moved, parts, acc, ends, sems, moves, side):
    columns = face.shape[1]
    groups = tiles.shape[0] // GROUP

    def tile_copy(g):
        part = pl.ds(g * GROUP, GROUP)
        return pltpu.make_async_copy(tiles.at[part], buf.at[part], sems.at[g])

    def pick(g):
        for i in range(GROUP):
            spot = slot[g * GROUP + i]
            place = spot & ((1 << SHIFT) - 1)
            pltpu.make_async_copy(
                arrived.at[spot >> SHIFT, pl.ds(pl.multiple_of(place * columns, 16), columns)],
                moved.at[g * GROUP + i],
                moves.at[g],
            ).start()

    for g in range(groups):
        pick(g)
        tile_copy(g).start()
    tail = pltpu.make_async_copy(arrived.at[:, pl.ds(ROOM * columns, META)], ends, side.at[0])
    tail.start()

    def arrive(g):
        held = moved.at[pl.ds(g * GROUP, GROUP)]
        pltpu.make_async_copy(held, held, moves.at[g]).wait()
        tile_copy(g).wait()

    def first(g):
        at = lax.rem(g, 2)
        for i in range(GROUP):
            p = g * GROUP + i
            parts[at, i] = lax.dot_general(
                moved[p], buf[p], (((1,), (1,)), ((), ())), preferred_element_type=jnp.float32
            )

    def second(g):
        at = lax.rem(g, 2)
        for i in range(GROUP):
            acc[fpatch[g * GROUP + i]] += parts[at, i]

    acc[...] = jnp.zeros_like(acc)
    stream(groups, arrive, first, second)
    out = pltpu.make_async_copy(acc, face, side.at[1])
    out.start()
    tail.wait()
    over[0] = jnp.max(ends[...].astype(jnp.float32)).astype(jnp.int32)
    out.wait()


def shards(disp, loads, tiles, pair_fpatch, pair_sdev, pair_spatch):
    n_wide = lax.axis_size("wide")
    n_narrow = lax.axis_size("narrow")
    pairs, faces, nodes = tiles.shape
    patches, columns, _ = disp.shape
    rows = ROOM * columns + META
    sdev = pair_sdev[:, 0]
    vmem = pl.BlockSpec(memory_space=pltpu.VMEM)
    smem = pl.BlockSpec(memory_space=pltpu.SMEM)
    hbm = pl.BlockSpec(memory_space=pltpu.HBM)
    tile_buf = pltpu.VMEM(tiles.shape, tiles.dtype)
    groups = pairs // GROUP
    part_buf = pltpu.VMEM((2, GROUP, columns, nodes), jnp.float32)
    dma = pltpu.SemaphoreType.DMA
    flops = 2 * pairs * columns * faces * nodes
    out, slot, aug = pl.pallas_call(
        functools.partial(send_kernel, n_narrow),
        out_shape=(
            jax.ShapeDtypeStruct((n_wide, rows, nodes), jnp.int16),
            jax.ShapeDtypeStruct((pairs,), jnp.int32),
            jax.ShapeDtypeStruct((patches + 1, columns, nodes), disp.dtype),
        ),
        in_specs=[smem, smem, smem, vmem, hbm, hbm],
        out_specs=(hbm, smem, hbm),
        scratch_shapes=[
            tile_buf,
            part_buf,
            pltpu.VMEM((2, GROUP, nodes), jnp.float32),
            pltpu.VMEM((GROUP, nodes), jnp.int32),
            pltpu.VMEM((pairs, columns, nodes), jnp.int16),
            pltpu.VMEM((n_wide, META, nodes), jnp.int32),
            pltpu.VMEM((n_wide, META, nodes), jnp.int16),
            pltpu.VMEM((patches + 1, columns, nodes), disp.dtype),
            pltpu.SMEM((n_wide,), jnp.int32),
            dma((groups,)),
            dma((3,)),
            dma,
        ],
        compiler_params=pltpu.CompilerParams(vmem_limit_bytes=LIMIT),
        cost_estimate=pl.CostEstimate(flops=flops, bytes_accessed=2 * tiles.size, transcendentals=0),
        name="send",
    )(pair_fpatch, sdev, pair_spatch, loads, tiles, disp)
    table = lax.all_gather(aug, "narrow", axis=0, tiled=True)
    arrived = lax.all_to_all(out, "wide", split_axis=0, concat_axis=0, tiled=True)
    answer, names = pl.pallas_call(
        functools.partial(pick_kernel, n_narrow),
        out_shape=(
            jax.ShapeDtypeStruct((n_wide, rows, nodes), disp.dtype),
            jax.ShapeDtypeStruct((n_wide, 128), jnp.int32),
        ),
        in_specs=[hbm, hbm],
        out_specs=(hbm, smem),
        scratch_shapes=[
            pltpu.VMEM((n_narrow * (patches + 1), columns, nodes), disp.dtype),
            pltpu.VMEM((n_wide, rows, nodes), disp.dtype),
            pltpu.VMEM((n_wide, META, nodes), jnp.int16),
            pltpu.VMEM((n_wide, 128), jnp.int32),
            dma((n_narrow,)),
            dma((n_wide,)),
            dma,
        ],
        compiler_params=pltpu.CompilerParams(vmem_limit_bytes=LIMIT),
        cost_estimate=pl.CostEstimate(flops=10**6, bytes_accessed=12 * 10**6, transcendentals=0),
        name="pick",
    )(arrived, table)
    back = lax.all_to_all(answer, "wide", split_axis=0, concat_axis=0, tiled=True)
    total = pl.pallas_call(
        functools.partial(total_kernel, n_narrow),
        out_shape=jax.ShapeDtypeStruct((n_narrow * patches, columns, nodes), jnp.float32),
        in_specs=[smem, hbm],
        out_specs=hbm,
        scratch_shapes=[
            pltpu.VMEM((n_wide, rows, nodes), jnp.int16),
            pltpu.VMEM((4, patches, columns, nodes), jnp.float32),
            pltpu.VMEM((n_wide, META, nodes), jnp.float32),
            pltpu.SMEM((n_narrow + 1, n_wide * ROOM + 1), jnp.int32),
            pltpu.SMEM((n_narrow + 1,), jnp.int32),
            dma((4,)),
            dma((4,)),
        ],
        compiler_params=pltpu.CompilerParams(vmem_limit_bytes=LIMIT),
        cost_estimate=pl.CostEstimate(flops=10**7, bytes_accessed=18 * 10**6, transcendentals=0),
        name="total",
    )(names, arrived)
    struct_loads = lax.psum_scatter(total, "narrow", scatter_dimension=0, tiled=True)
    face_disp, over = pl.pallas_call(
        face_kernel,
        out_shape=(
            jax.ShapeDtypeStruct((loads.shape[0], columns, faces), jnp.float32),
            jax.ShapeDtypeStruct((1,), jnp.int32),
        ),
        in_specs=[smem, smem, hbm, hbm],
        out_specs=(hbm, smem),
        scratch_shapes=[
            tile_buf,
            pltpu.VMEM((pairs, columns, nodes), disp.dtype),
            part_buf,
            pltpu.VMEM((loads.shape[0], columns, faces), jnp.float32),
            pltpu.VMEM((n_wide, META, nodes), disp.dtype),
            dma((groups,)),
            dma((groups,)),
            dma((2,)),
        ],
        compiler_params=pltpu.CompilerParams(vmem_limit_bytes=LIMIT),
        cost_estimate=pl.CostEstimate(flops=flops, bytes_accessed=2 * tiles.size, transcendentals=0),
        name="face",
    )(pair_fpatch, slot, back, tiles)
    return lax.cond(
        over[0] > ROOM,
        lambda f, s: long_way(disp, loads, tiles, pair_fpatch, sdev, pair_spatch),
        lambda f, s: (f, s),
        face_disp,
        struct_loads,
    )


def solution(mesh):
    placed = (
        P(("wide", "narrow"), None, None),
        P(("wide", "narrow"), None, None),
        P(("wide", "narrow"), None, None),
        P(("wide", "narrow")),
        P(("wide", "narrow"), None),
        P(("wide", "narrow")),
    )
    return jax.shard_map(
        shards,
        mesh=mesh,
        in_specs=placed,
        out_specs=(P(("wide", "narrow"), None, None), P(("wide", "narrow"), None, None)),
        check_vma=False,
    )
```

profile of v0, /device:TPU:108, one launch (start us, length us, event | category | flops | bytes accessed | tf_op | source)
XLA Modules:
  0.0 185.1 jit_solution(13680324750656746922)
XLA Ops:
  7.2 0.0 all-gather.2.cloned.1.call-start
  7.2 9.9 %send.1 = (s16[16,592,256]{2,1,0:T(8,128)(2,1)}, s32[128]{0:T(128)}, bf16[33,48,256]{2,1,0:T(8,128)(2,1)}) custom-call(s32[128]{0:T(128)} %fpatch.3, s32[128]{0:T(128)} %bitcast.43, s32[128]{0:T(128)} %spatch.1, bf16[32,48,256]{2,1,0:T(8,128)(2,1)} %loads.1, bf16[128,256,256]{2,1,0:T(8,128)(2,1)} %tiles.3, bf16[32,48,256]{2,1,0:T(8,128)(2,1)} %disp.1), custom_call_target="tpu_custom_call" | custom-call | flops 805306368 | bytes 16777216 | tf_op jit(solution)/shard_map/send/pallas_call | solution.py:329
  17.1 0.0 all-gather.2.cloned.1.call-update
  17.2 0.0 reduce-scatter.2.cloned.1.call-start
  17.2 61.8 %all_to_all.24.arrived = s16[16,592,256]{2,1,0:T(8,128)(2,1)} all-to-all(s16[16,592,256]{2,1,0:T(8,128)(2,1)} %get-tuple-element.35), channel_id=1, replica_groups=mesh['wide'=16,'narrow'=8] {'wide'}, dimensions={0} | all-to-all | bytes 9699328 | tf_op jit(solution)/shard_map/all_to_all | solution.py:357
  79.0 0.0 all-gather.2.cloned.1.call-done.table
  79.0 6.4 %pick.1 = (bf16[16,592,256]{2,1,0:T(8,128)(2,1)}, s32[16,128]{1,0:T(8,128)}) custom-call(s16[16,592,256]{2,1,0:T(8,128)(2,1)} %all_to_all.24.arrived, bf16[264,48,256]{2,1,0:T(8,128)(2,1)} %all-gather.2.cloned.1.call-done.table), custom_call_target="tpu_custom_call" | custom-call | flops 1000000 | bytes 12000000 | tf_op jit(solution)/shard_map/pick/pallas_call | solution.py:358
  85.4 8.1 %total.1 = f32[256,48,256]{2,1,0:T(8,128)} custom-call(s32[16,128]{1,0:T(8,128)} %get-tuple-element.40.names, s16[16,592,256]{2,1,0:T(8,128)(2,1)} %all_to_all.24.arrived), custom_call_target="tpu_custom_call" | custom-call | flops 10000000 | bytes 18000000 | tf_op jit(solution)/shard_map/total/pallas_call | solution.py:380
  93.5 0.0 reduce-scatter.2.cloned.1.call-update
  93.5 0.0 copy-start.2
  93.5 8.1 %all-to-all-start.4 = ((bf16[16,592,256]{2,1,0:T(8,128)(2,1)}), bf16[16,592,256]{2,1,0:T(8,128)(2,1)}, u32[]{:S(2)}, u32[]{:S(2)}) async-start(bf16[16,592,256]{2,1,0:T(8,128)(2,1)} %get-tuple-element.37), calls=%async_computation.4 | async-start | bytes 9699328 | tf_op jit(solution)/shard_map/all_to_all | solution.py:379
  101.6 64.2 %all-to-all-done.4.arrived = bf16[16,592,256]{2,1,0:T(8,128)(2,1)} async-done(((bf16[16,592,256]{2,1,0:T(8,128)(2,1)}), bf16[16,592,256]{2,1,0:T(8,128)(2,1)}, u32[]{:S(2)}, u32[]{:S(2)}) %all-to-all-start.4) | async-done | bytes 4849696 | tf_op jit(solution)/shard_map/all_to_all | solution.py:379
  165.8 0.0 copy-done.2
  165.8 0.0 copy-start
  165.8 0.0 copy-start.1
  165.8 0.0 copy-start.3
  165.8 11.6 %face.1 = (f32[32,48,256]{2,1,0:T(8,128)}, s32[1]{0:T(128)}) custom-call(s32[128]{0:T(128)S(1)} %copy-done.2, s32[128]{0:T(128)} %get-tuple-element.34.slot, bf16[16,592,256]{2,1,0:T(8,128)(2,1)} %all-to-all-done.4.arrived, bf16[128,256,256]{2,1,0:T(8,128)(2,1)} %tiles.3), custom_call_target="tpu_custom_call" | custom-call | flops 805306368 | bytes 16777216 | tf_op jit(solution)/shard_map/face/pallas_call | solution.py:399
  177.9 0.0 reduce-scatter.2.cloned.1.call-done
  178.0 0.0 copy-done
  178.0 0.0 copy-done.1
  178.0 0.0 copy-done.3
  178.0 0.2 conditional.1
Async XLA Ops:
  7.2 71.9 %all-gather.2.cloned.1.call-start = ((), (), s32[]{:S(2)}) async-start(), calls=%async_computation.6 | async-start | bytes 7299072 | tf_op jit(solution)/shard_map/all_gather | solution.py:356
  17.2 160.8 %reduce-scatter.2.cloned.1.call-start = ((), (), s32[]{:S(2)}) async-start(), calls=%async_computation.7 | async-start | bytes 14155776 | tf_op jit(solution)/shard_map/reduce_scatter | solution.py:398
  93.5 72.3 %copy-start.2 = (s32[128]{0:T(128)S(1)}, s32[128]{0:T(128)}, u32[]{:S(2)}) copy-start(s32[128]{0:T(128)} %fpatch.3) | copy-start | bytes 1540
  93.5 72.3 %all-to-all-start.4 = ((bf16[16,592,256]{2,1,0:T(8,128)(2,1)}), bf16[16,592,256]{2,1,0:T(8,128)(2,1)}, u32[]{:S(2)}, u32[]{:S(2)}) async-start(bf16[16,592,256]{2,1,0:T(8,128)(2,1)} %get-tuple-element.37), calls=%async_computation.4 | async-start | bytes 9699328 | tf_op jit(solution)/shard_map/all_to_all | solution.py:379
  165.8 12.2 %copy-start = (s32[128]{0:T(128)S(1)}, s32[128]{0:T(128)}, u32[]{:S(2)}) copy-start(s32[128]{0:T(128)} %spatch.1) | copy-start | bytes 1540
  165.8 12.2 %copy-start.1 = (bf16[32,48,256]{2,1,0:T(8,128)(2,1)S(1)}, bf16[32,48,256]{2,1,0:T(8,128)(2,1)}, u32[]{:S(2)}) copy-start(bf16[32,48,256]{2,1,0:T(8,128)(2,1)} %disp.1) | copy-start | bytes 2359300
  165.8 12.2 %copy-start.3 = (s32[128,1]{0,1:T(1,128)S(1)}, s32[128,1]{0,1:T(1,128)}, u32[]{:S(2)}) copy-start(s32[128,1]{0,1:T(1,128)} %param.12) | copy-start | bytes 1540
Sparse Core Ops, SparseCore 0:
  17.3 41.9 all-gather.1
  93.6 71.6 reduce-scatter.1
where the time goes:
time: 186 us; the launch traced here: 185 us
  waiting for transfers between devices  64.2 us (35%)
  blocking collectives  61.8 us (33%)
  Pallas kernels  35.9 us (19%)
  between operations  14.7 us (8%)
  starting transfers between devices  8.21 us (4%)
    all_to_all x1, waiting for transfers between devices, shards(): lax.all_to_all(answer, 'wide', split_axis=0, concat_axis=0, tiled=True)  64.2 us
    all_to_all x1, blocking collectives, shards(): lax.all_to_all(out, 'wide', split_axis=0, concat_axis=0, tiled=True)  61.8 us
    pallas_call x1, Pallas kernels, shards(): pl.pallas_call(face_kernel, out_shape=(jax.ShapeDtypeStruct((loads.shape[...  11.6 us
    pallas_call x1, Pallas kernels, shards(): pl.pallas_call(functools.partial(send_kernel, n_narrow), out_shape=(jax.S...  9.93 us
    all_to_all x1, starting transfers between devices, shards(): lax.all_to_all(answer, 'wide', split_axis=0, concat_axis=0, tiled=True)  8.13 us
    pallas_call x1, Pallas kernels, shards(): pl.pallas_call(functools.partial(total_kernel, n_narrow), out_shape=jax.S...  8.05 us
    pallas_call x1, Pallas kernels, shards(): pl.pallas_call(functools.partial(pick_kernel, n_narrow), out_shape=(jax.S...  6.37 us
  transfers between devices with their start and end apart: 3, of which 1 were waited for; matrix products, arithmetic and copies ran while one was open for 0% of the time, Pallas kernels for 6%

commit v1 on v0

--- a/solution.py
+++ b/solution.py
@@ -11,6 +11,7 @@
 META = 16
 SHIFT = 4
 GROUP = 16
+AHEAD = 4
 STEPS = 128.0
 TOP = 32760.0
 LIMIT = 63 << 20
@@ -72,18 +73,9 @@
     return (face_disp, struct_loads)
 
 
-def stream(groups, arrive, first, second):
-    arrive(0)
-    first(0)
-
-    def step(g, carry):
-        arrive(g)
-        first(g)
-        second(g - 1)
-        return carry
-
-    lax.fori_loop(1, groups, step, 0)
-    second(groups - 1)
+def tile_copy(tiles, buf, sems, g):
+    part = pl.ds(g * GROUP, GROUP)
+    return pltpu.make_async_copy(tiles.at[part], buf.at[part], sems.at[g])
 
 
 def send_kernel(
@@ -94,12 +86,8 @@
     groups = tiles.shape[0] // GROUP
     groups = tiles.shape[0] // GROUP
 
-    def tile_copy(g):
-        part = pl.ds(g * GROUP, GROUP)
-        return pltpu.make_async_copy(tiles.at[part], buf.at[part], sems.at[g])
-
     for g in range(groups):
-        tile_copy(g).start()
+        tile_copy(tiles, buf, sems, g).start()
     keep = pltpu.make_async_copy(disp, own.at[pl.ds(0, patches)], side.at[0])
     keep.start()
     meta[...] = jnp.zeros_like(meta)
@@ -139,7 +127,18 @@
             names = meta[w, ROOM : ROOM + 1, :]
             meta[w, ROOM : ROOM + 1, :] = jnp.where(lane == place, asked, names)
 
-    stream(groups, lambda g: tile_copy(g).wait(), first, second)
+
+    tile_copy(tiles, buf, sems, 0).wait()
+    first(0)
+
+    def step(g, carry):
+        tile_copy(tiles, buf, sems, g).wait()
+        first(g)
+        second(g - 1)
+        return carry
+
+    lax.fori_loop(1, groups, step, 0)
+    second(groups - 1)
     ends[...] = meta[...].astype(jnp.int16)
     tail = pltpu.make_async_copy(ends, out.at[:, pl.ds(ROOM * columns, META)], side.at[1])
     tail.start()
@@ -155,24 +154,39 @@
     mark.wait()
 
 
-def pick_kernel(n_narrow, arrived, table, answer, names, held, gone, meta, wide_names, coming, outs, side):
+def turn_kernel(
+    n_narrow, arrived, table, total, answer,
+    held, gone, came, acc, scale, meta, wide_names, names, lists, count, tables, comes, goes, outs, side,
+):
     n_wide, columns = arrived.shape[0], table.shape[1]
     stride = table.shape[0] // n_narrow
     patches = stride - 1
+    quarter = n_wide // 4
     ends = pltpu.make_async_copy(arrived.at[:, pl.ds(ROOM * columns, META)], meta, side)
     ends.start()
     loading = [
         pltpu.make_async_copy(
-            table.at[pl.ds(b * stride, stride)], held.at[pl.ds(b * stride, stride)], coming.at[b]
+            table.at[pl.ds(b * stride, stride)], held.at[pl.ds(b * stride, stride)], tables.at[b]
         )
         for b in range(n_narrow)
     ]
-    for each in loading:
+    coming = [
+        pltpu.make_async_copy(
+            arrived.at[pl.ds(i * quarter, quarter)], came.at[pl.ds(i * quarter, quarter)], comes.at[i]
+        )
+        for i in range(4)
+    ]
+    for each in loading + coming:
         each.start()
+    for b in range(n_narrow + 1):
+        count[b] = 0
     ends.wait()
     wide_names[...] = meta[...].astype(jnp.int32)[:, ROOM, : wide_names.shape[1]]
     naming = pltpu.make_async_copy(wide_names, names, side)
     naming.start()
+    scale[...] = jnp.exp2(meta[...].astype(jnp.int32).astype(jnp.float32) * (1.0 / STEPS)) * (1.0 / TOP)
+    scale[0, META - 1 : META, :] = jnp.zeros((1, scale.shape[2]), jnp.float32)
+    acc[...] = jnp.zeros_like(acc)
     for each in loading:
         each.wait()
     fullest = held[patches, 0:META, :].astype(jnp.float32)
@@ -181,55 +195,27 @@
     gone[:, ROOM * columns :, :] = jnp.broadcast_to(fullest, (n_wide,) + fullest.shape).astype(gone.dtype)
     naming.wait()
 
-    def leave(w):
-        return pltpu.make_async_copy(gone.at[w], answer.at[w], outs.at[w])
+    def away(w):
+        return pltpu.make_async_copy(gone.at[w], answer.at[w], goes.at[w])
 
     def send(w, carry):
         for j in range(ROOM):
-            name = jnp.maximum(names[w, j], 0)
-            gone[w, j * columns : (j + 1) * columns, :] = held[name + lax.div(name, patches)]
-        leave(w).start()
-        return carry
-
-    lax.fori_loop(0, n_wide, send, 0)
-    for w in range(n_wide):
-        leave(w).wait()
-
-
-def total_kernel(n_narrow, names, arrived, total, came, acc, scale, lists, count, coming, outs):
-    n_wide, columns = arrived.shape[0], total.shape[1]
-    patches = total.shape[0] // n_narrow
-    quarter = n_wide // 4
-    loading = [
-        pltpu.make_async_copy(
-            arrived.at[pl.ds(i * quarter, quarter)], came.at[pl.ds(i * quarter, quarter)], coming.at[i]
-        )
-        for i in range(4)
-    ]
-    for each in loading:
-        each.start()
-    for b in range(n_narrow + 1):
-        count[b] = 0
-
-    def file(w, carry):
-        for j in range(ROOM):
             name = names[w, j]
-            held = jnp.maximum(name, 0)
-            b = lax.div(held, patches)
+            asked = jnp.maximum(name, 0)
+            b = lax.div(asked, patches)
+            gone[w, j * columns : (j + 1) * columns, :] = held[asked + b]
             chosen = jnp.where(name >= 0, b, n_narrow)
             k = count[chosen]
             count[chosen] = k + 1
-            lists[chosen, k] = (w << 16) | (j << 12) | (j << 8) | (held - b * patches)
+            lists[chosen, k] = (w << 16) | (j << 12) | (j << 8) | (asked - b * patches)
+        away(w).start()
         return carry
 
-    lax.fori_loop(0, n_wide, file, 0)
+    lax.fori_loop(0, n_wide, send, 0)
     for b in range(n_narrow):
         lists[b, count[b]] = (META - 1) << 8
-    acc[...] = jnp.zeros_like(acc)
-    for each in loading:
+    for each in coming:
         each.wait()
-    scale[...] = jnp.exp2(came[:, ROOM * columns :, :].astype(jnp.int32).astype(jnp.float32) * (1.0 / STEPS)) * (1.0 / TOP)
-    scale[0, META - 1 : META, :] = jnp.zeros((1, scale.shape[2]), jnp.float32)
 
     def leave(b):
         return pltpu.make_async_copy(acc.at[b % 4], total.at[pl.ds(b * patches, patches)], outs.at[b % 4])
@@ -256,19 +242,17 @@
 
         lax.fori_loop(0, lax.div(count[b] + 1, 2), add, 0)
         leave(b).start()
+    for w in range(n_wide):
+        away(w).wait()
     for b in range(n_narrow - 4, n_narrow):
         leave(b).wait()
 
 
-def face_kernel(fpatch, slot, arrived, tiles, face, over, buf, moved, parts, acc, ends, sems, moves, side):
+def face_kernel(fpatch, slot, arrived, tiles, face, over, buf, moved, acc, ends, sems, moves, side):
     columns = face.shape[1]
     groups = tiles.shape[0] // GROUP
 
-    def tile_copy(g):
-        part = pl.ds(g * GROUP, GROUP)
-        return pltpu.make_async_copy(tiles.at[part], buf.at[part], sems.at[g])
-
-    def pick(g):
+    def fetch(g):
         for i in range(GROUP):
             spot = slot[g * GROUP + i]
             place = spot & ((1 << SHIFT) - 1)
@@ -277,33 +261,31 @@
                 moved.at[g * GROUP + i],
                 moves.at[g],
             ).start()
-
-    for g in range(groups):
-        pick(g)
-        tile_copy(g).start()
+        tile_copy(tiles, buf, sems, g).start()
+
+    for g in range(AHEAD):
+        fetch(g)
     tail = pltpu.make_async_copy(arrived.at[:, pl.ds(ROOM * columns, META)], ends, side.at[0])
     tail.start()
-
-    def arrive(g):
+    acc[...] = jnp.zeros_like(acc)
+
+    def step(g, carry):
         held = moved.at[pl.ds(g * GROUP, GROUP)]
         pltpu.make_async_copy(held, held, moves.at[g]).wait()
-        tile_copy(g).wait()
-
-    def first(g):
-        at = lax.rem(g, 2)
+        tile_copy(tiles, buf, sems, g).wait()
+
+        @pl.when(g + AHEAD < groups)
+        def _():
+            fetch(g + AHEAD)
+
         for i in range(GROUP):
             p = g * GROUP + i
-            parts[at, i] = lax.dot_general(
+            acc[fpatch[p]] += lax.dot_general(
                 moved[p], buf[p], (((1,), (1,)), ((), ())), preferred_element_type=jnp.float32
             )
-
-    def second(g):
-        at = lax.rem(g, 2)
-        for i in range(GROUP):
-            acc[fpatch[g * GROUP + i]] += parts[at, i]
-
-    acc[...] = jnp.zeros_like(acc)
-    stream(groups, arrive, first, second)
+        return carry
+
+    lax.fori_loop(0, groups, step, 0)
     out = pltpu.make_async_copy(acc, face, side.at[1])
     out.start()
     tail.wait()
@@ -355,46 +337,36 @@
     )(pair_fpatch, sdev, pair_spatch, loads, tiles, disp)
     table = lax.all_gather(aug, "narrow", axis=0, tiled=True)
     arrived = lax.all_to_all(out, "wide", split_axis=0, concat_axis=0, tiled=True)
-    answer, names = pl.pallas_call(
-        functools.partial(pick_kernel, n_narrow),
+    total, answer = pl.pallas_call(
+        functools.partial(turn_kernel, n_narrow),
         out_shape=(
+            jax.ShapeDtypeStruct((n_narrow * patches, columns, nodes), jnp.float32),
             jax.ShapeDtypeStruct((n_wide, rows, nodes), disp.dtype),
-            jax.ShapeDtypeStruct((n_wide, 128), jnp.int32),
         ),
         in_specs=[hbm, hbm],
-        out_specs=(hbm, smem),
+        out_specs=(hbm, hbm),
         scratch_shapes=[
             pltpu.VMEM((n_narrow * (patches + 1), columns, nodes), disp.dtype),
             pltpu.VMEM((n_wide, rows, nodes), disp.dtype),
+            pltpu.VMEM((n_wide, rows, nodes), jnp.int16),
+            pltpu.VMEM((4, patches, columns, nodes), jnp.float32),
+            pltpu.VMEM((n_wide, META, nodes), jnp.float32),
             pltpu.VMEM((n_wide, META, nodes), jnp.int16),
             pltpu.VMEM((n_wide, 128), jnp.int32),
+            pltpu.SMEM((n_wide, 128), jnp.int32),
+            pltpu.SMEM((n_narrow + 1, n_wide * ROOM + 1), jnp.int32),
+            pltpu.SMEM((n_narrow + 1,), jnp.int32),
             dma((n_narrow,)),
+            dma((4,)),
             dma((n_wide,)),
+            dma((4,)),
             dma,
         ],
         compiler_params=pltpu.CompilerParams(vmem_limit_bytes=LIMIT),
-        cost_estimate=pl.CostEstimate(flops=10**6, bytes_accessed=12 * 10**6, transcendentals=0),
-        name="pick",
+        cost_estimate=pl.CostEstimate(flops=10**7, bytes_accessed=29 * 10**6, transcendentals=0),
+        name="turn",
     )(arrived, table)
     back = lax.all_to_all(answer, "wide", split_axis=0, concat_axis=0, tiled=True)
-    total = pl.pallas_call(
-        functools.partial(total_kernel, n_narrow),
-        out_shape=jax.ShapeDtypeStruct((n_narrow * patches, columns, nodes), jnp.float32),
-        in_specs=[smem, hbm],
-        out_specs=hbm,
-        scratch_shapes=[
-            pltpu.VMEM((n_wide, rows, nodes), jnp.int16),
-            pltpu.VMEM((4, patches, columns, nodes), jnp.float32),
-            pltpu.VMEM((n_wide, META, nodes), jnp.float32),
-            pltpu.SMEM((n_narrow + 1, n_wide * ROOM + 1), jnp.int32),
-            pltpu.SMEM((n_narrow + 1,), jnp.int32),
-            dma((4,)),
-            dma((4,)),
-        ],
-        compiler_params=pltpu.CompilerParams(vmem_limit_bytes=LIMIT),
-        cost_estimate=pl.CostEstimate(flops=10**7, bytes_accessed=18 * 10**6, transcendentals=0),
-        name="total",
-    )(names, arrived)
     struct_loads = lax.psum_scatter(total, "narrow", scatter_dimension=0, tiled=True)
     face_disp, over = pl.pallas_call(
         face_kernel,
@@ -407,7 +379,6 @@
         scratch_shapes=[
             tile_buf,
             pltpu.VMEM((pairs, columns, nodes), disp.dtype),
-            part_buf,
             pltpu.VMEM((loads.shape[0], columns, faces), jnp.float32),
             pltpu.VMEM((n_wide, META, nodes), disp.dtype),
             dma((groups,)),

time: 186 us -> 183 us (0.984)
  Pallas kernels: 35.9 us -> 32.4 us
    pallas_call x2 -> x1, Pallas kernels: 14.4 us -> 11.5 us  [shards(): pl.pallas_call(functools.partial(turn_kernel, n_narrow), out_shape=(jax.S...]
where the time goes in v1:
time: 183 us
  waiting for transfers between devices  65.3 us (36%)
  blocking collectives  61.8 us (34%)
  Pallas kernels  32.4 us (18%)
  between operations  14.7 us (8%)
  starting transfers between devices  8.15 us (4%)
    all_to_all x1, waiting for transfers between devices, shards(): lax.all_to_all(answer, 'wide', split_axis=0, concat_axis=0, tiled=True)  65.2 us
    all_to_all x1, blocking collectives, shards(): lax.all_to_all(out, 'wide', split_axis=0, concat_axis=0, tiled=True)  61.8 us
    pallas_call x1, Pallas kernels, shards(): pl.pallas_call(functools.partial(turn_kernel, n_narrow), out_shape=(jax.S...  11.5 us
    pallas_call x1, Pallas kernels, shards(): pl.pallas_call(face_kernel, out_shape=(jax.ShapeDtypeStruct((loads.shape[...  11 us
    pallas_call x1, Pallas kernels, shards(): pl.pallas_call(functools.partial(send_kernel, n_narrow), out_shape=(jax.S...  9.93 us
    all_to_all x1, starting transfers between devices, shards(): lax.all_to_all(answer, 'wide', split_axis=0, concat_axis=0, tiled=True)  8.07 us
  transfers between devices with their start and end apart: 3, of which 1 were waited for; matrix products, arithmetic and copies ran while one was open for 0% of the time, Pallas kernels for 6%

profile of v1, /device:TPU:108, one launch (start us, length us, event | category | flops | bytes accessed | tf_op | source)
XLA Modules:
  0.0 182.6 jit_solution(17189935521794149330)
XLA Ops:
  7.2 0.0 all-gather.2.cloned.1.call-start
  7.2 9.9 %send.1 = (s16[16,592,256]{2,1,0:T(8,128)(2,1)}, s32[128]{0:T(128)}, bf16[33,48,256]{2,1,0:T(8,128)(2,1)}) custom-call(s32[128]{0:T(128)} %fpatch.3, s32[128]{0:T(128)} %bitcast.43, s32[128]{0:T(128)} %spatch.1, bf16[32,48,256]{2,1,0:T(8,128)(2,1)} %loads.1, bf16[128,256,256]{2,1,0:T(8,128)(2,1)} %tiles.3, bf16[32,48,256]{2,1,0:T(8,128)(2,1)} %disp.1), custom_call_target="tpu_custom_call" | custom-call | flops 805306368 | bytes 16777216 | tf_op jit(solution)/shard_map/send/pallas_call | solution.py:311
  17.1 0.0 all-gather.2.cloned.1.call-update
  17.2 0.0 reduce-scatter.2.cloned.1.call-start
  17.2 61.8 %all_to_all.24.arrived = s16[16,592,256]{2,1,0:T(8,128)(2,1)} all-to-all(s16[16,592,256]{2,1,0:T(8,128)(2,1)} %get-tuple-element.35), channel_id=1, replica_groups=mesh['wide'=16,'narrow'=8] {'wide'}, dimensions={0} | all-to-all | bytes 9699328 | tf_op jit(solution)/shard_map/all_to_all | solution.py:339
  79.0 0.0 all-gather.2.cloned.1.call-done.table
  79.0 11.5 %turn.1 = (f32[256,48,256]{2,1,0:T(8,128)}, bf16[16,592,256]{2,1,0:T(8,128)(2,1)}) custom-call(s16[16,592,256]{2,1,0:T(8,128)(2,1)} %all_to_all.24.arrived, bf16[264,48,256]{2,1,0:T(8,128)(2,1)} %all-gather.2.cloned.1.call-done.table), custom_call_target="tpu_custom_call" | custom-call | flops 10000000 | bytes 29000000 | tf_op jit(solution)/shard_map/turn/pallas_call | solution.py:340
  90.5 0.0 reduce-scatter.2.cloned.1.call-update
  90.5 0.0 copy-start.2
  90.5 8.1 %all-to-all-start.4 = ((bf16[16,592,256]{2,1,0:T(8,128)(2,1)}), bf16[16,592,256]{2,1,0:T(8,128)(2,1)}, u32[]{:S(2)}, u32[]{:S(2)}) async-start(bf16[16,592,256]{2,1,0:T(8,128)(2,1)} %get-tuple-element.37), calls=%async_computation.4 | async-start | bytes 9699328 | tf_op jit(solution)/shard_map/all_to_all | solution.py:369
  98.6 65.2 %all-to-all-done.4.arrived = bf16[16,592,256]{2,1,0:T(8,128)(2,1)} async-done(((bf16[16,592,256]{2,1,0:T(8,128)(2,1)}), bf16[16,592,256]{2,1,0:T(8,128)(2,1)}, u32[]{:S(2)}, u32[]{:S(2)}) %all-to-all-start.4) | async-done | bytes 4849696 | tf_op jit(solution)/shard_map/all_to_all | solution.py:369
  163.9 0.0 copy-done.2
  163.9 0.0 copy-start
  163.9 0.0 copy-start.1
  163.9 0.0 copy-start.3
  163.9 11.0 %face.1 = (f32[32,48,256]{2,1,0:T(8,128)}, s32[1]{0:T(128)}) custom-call(s32[128]{0:T(128)S(1)} %copy-done.2, s32[128]{0:T(128)} %get-tuple-element.34.slot, bf16[16,592,256]{2,1,0:T(8,128)(2,1)} %all-to-all-done.4.arrived, bf16[128,256,256]{2,1,0:T(8,128)(2,1)} %tiles.3), custom_call_target="tpu_custom_call" | custom-call | flops 805306368 | bytes 16777216 | tf_op jit(solution)/shard_map/face/pallas_call | solution.py:371
  175.4 0.0 reduce-scatter.2.cloned.1.call-done
  175.5 0.0 copy-done
  175.5 0.0 copy-done.1
  175.5 0.0 copy-done.3
  175.5 0.2 conditional.1
Async XLA Ops:
  7.2 71.9 %all-gather.2.cloned.1.call-start = ((), (), s32[]{:S(2)}) async-start(), calls=%async_computation.6 | async-start | bytes 7299072 | tf_op jit(solution)/shard_map/all_gather | solution.py:338
  17.2 158.3 %reduce-scatter.2.cloned.1.call-start = ((), (), s32[]{:S(2)}) async-start(), calls=%async_computation.7 | async-start | bytes 14155776 | tf_op jit(solution)/shard_map/reduce_scatter | solution.py:370
  90.5 73.3 %copy-start.2 = (s32[128]{0:T(128)S(1)}, s32[128]{0:T(128)}, u32[]{:S(2)}) copy-start(s32[128]{0:T(128)} %fpatch.3) | copy-start | bytes 1540
  90.5 73.3 %all-to-all-start.4 = ((bf16[16,592,256]{2,1,0:T(8,128)(2,1)}), bf16[16,592,256]{2,1,0:T(8,128)(2,1)}, u32[]{:S(2)}, u32[]{:S(2)}) async-start(bf16[16,592,256]{2,1,0:T(8,128)(2,1)} %get-tuple-element.37), calls=%async_computation.4 | async-start | bytes 9699328 | tf_op jit(solution)/shard_map/all_to_all | solution.py:369
  163.9 11.6 %copy-start = (s32[128]{0:T(128)S(1)}, s32[128]{0:T(128)}, u32[]{:S(2)}) copy-start(s32[128]{0:T(128)} %spatch.1) | copy-start | bytes 1540
  163.9 11.6 %copy-start.1 = (bf16[32,48,256]{2,1,0:T(8,128)(2,1)S(1)}, bf16[32,48,256]{2,1,0:T(8,128)(2,1)}, u32[]{:S(2)}) copy-start(bf16[32,48,256]{2,1,0:T(8,128)(2,1)} %disp.1) | copy-start | bytes 2359300
  163.9 11.6 %copy-start.3 = (s32[128,1]{0,1:T(1,128)S(1)}, s32[128,1]{0,1:T(1,128)}, u32[]{:S(2)}) copy-start(s32[128,1]{0,1:T(1,128)} %param.12) | copy-start | bytes 1540
Sparse Core Ops, SparseCore 0:
  17.3 41.9 all-gather.1
  90.7 71.9 reduce-scatter.1

commit v2 on v1

--- a/solution.py
+++ b/solution.py
@@ -14,6 +14,7 @@
 AHEAD = 4
 STEPS = 128.0
 TOP = 32760.0
+MARK = 1e37
 LIMIT = 63 << 20
 
 
@@ -79,17 +80,15 @@
 
 
 def send_kernel(
-    n_narrow, fpatch, sdev, spatch, loads, tiles, disp, out, slot, aug,
-    buf, parts, most, power, whole, meta, ends, own, count, sems, side, leaving,
+    n_narrow, patches, fpatch, sdev, spatch, loads, tiles, out, slot,
+    buf, parts, most, power, whole, meta, ends, count, sems, side, leaving,
 ):
-    n_wide, patches, columns = out.shape[0], disp.shape[0], disp.shape[1]
+    n_wide, columns = out.shape[0], whole.shape[1]
     groups = tiles.shape[0] // GROUP
     groups = tiles.shape[0] // GROUP
 
     for g in range(groups):
         tile_copy(tiles, buf, sems, g).start()
-    keep = pltpu.make_async_copy(disp, own.at[pl.ds(0, patches)], side.at[0])
-    keep.start()
     meta[...] = jnp.zeros_like(meta)
     for w in range(n_wide):
         count[w] = 0
@@ -139,19 +138,17 @@
 
     lax.fori_loop(1, groups, step, 0)
     second(groups - 1)
-    ends[...] = meta[...].astype(jnp.int16)
-    tail = pltpu.make_async_copy(ends, out.at[:, pl.ds(ROOM * columns, META)], side.at[1])
-    tail.start()
     fullest = count[0]
     for w in range(1, n_wide):
         fullest = jnp.maximum(fullest, count[w])
-    own[patches] = jnp.full(own.shape[1:], fullest.astype(jnp.float32), jnp.float32).astype(own.dtype)
-    keep.wait()
-    mark = pltpu.make_async_copy(own, aug, side.at[2])
-    mark.start()
+    for w in range(n_wide):
+        names = meta[w, ROOM : ROOM + 1, :]
+        meta[w, ROOM : ROOM + 1, :] = jnp.where(lane == ROOM, fullest, names)
+    ends[...] = meta[...].astype(jnp.int16)
+    tail = pltpu.make_async_copy(ends, out.at[:, pl.ds(ROOM * columns, META)], side)
+    tail.start()
     pltpu.make_async_copy(whole, whole, leaving).wait()
     tail.wait()
-    mark.wait()
 
 
 def turn_kernel(
@@ -159,14 +156,13 @@
     held, gone, came, acc, scale, meta, wide_names, names, lists, count, tables, comes, goes, outs, side,
 ):
     n_wide, columns = arrived.shape[0], table.shape[1]
-    stride = table.shape[0] // n_narrow
-    patches = stride - 1
+    patches = table.shape[0] // n_narrow
     quarter = n_wide // 4
     ends = pltpu.make_async_copy(arrived.at[:, pl.ds(ROOM * columns, META)], meta, side)
     ends.start()
     loading = [
         pltpu.make_async_copy(
-            table.at[pl.ds(b * stride, stride)], held.at[pl.ds(b * stride, stride)], tables.at[b]
+            table.at[pl.ds(b * patches, patches)], held.at[pl.ds(b * patches, patches)], tables.at[b]
         )
         for b in range(n_narrow)
     ]
@@ -189,10 +185,6 @@
     acc[...] = jnp.zeros_like(acc)
     for each in loading:
         each.wait()
-    fullest = held[patches, 0:META, :].astype(jnp.float32)
-    for b in range(1, n_narrow):
-        fullest = jnp.maximum(fullest, held[b * stride + patches, 0:META, :].astype(jnp.float32))
-    gone[:, ROOM * columns :, :] = jnp.broadcast_to(fullest, (n_wide,) + fullest.shape).astype(gone.dtype)
     naming.wait()
 
     def away(w):
@@ -203,7 +195,7 @@
             name = names[w, j]
             asked = jnp.maximum(name, 0)
             b = lax.div(asked, patches)
-            gone[w, j * columns : (j + 1) * columns, :] = held[asked + b]
+            gone[w, j * columns : (j + 1) * columns, :] = held[asked]
             chosen = jnp.where(name >= 0, b, n_narrow)
             k = count[chosen]
             count[chosen] = k + 1
@@ -212,6 +204,10 @@
         return carry
 
     lax.fori_loop(0, n_wide, send, 0)
+    fullest = names[0, ROOM]
+    for w in range(1, n_wide):
+        fullest = jnp.maximum(fullest, names[w, ROOM])
+    mark = jnp.where(fullest > ROOM, MARK, 0.0)
     for b in range(n_narrow):
         lists[b, count[b]] = (META - 1) << 8
     for each in coming:
@@ -241,6 +237,7 @@
             return carry
 
         lax.fori_loop(0, lax.div(count[b] + 1, 2), add, 0)
+        acc[at, 0, 0:8, 0:128] += jnp.full((8, 128), mark, jnp.float32)
         leave(b).start()
     for w in range(n_wide):
         away(w).wait()
@@ -248,7 +245,7 @@
         leave(b).wait()
 
 
-def face_kernel(fpatch, slot, arrived, tiles, face, over, buf, moved, acc, ends, sems, moves, side):
+def face_kernel(fpatch, slot, arrived, tiles, face, buf, moved, acc, sems, moves, side):
     columns = face.shape[1]
     groups = tiles.shape[0] // GROUP
 
@@ -265,8 +262,6 @@
 
     for g in range(AHEAD):
         fetch(g)
-    tail = pltpu.make_async_copy(arrived.at[:, pl.ds(ROOM * columns, META)], ends, side.at[0])
-    tail.start()
     acc[...] = jnp.zeros_like(acc)
 
     def step(g, carry):
@@ -286,10 +281,8 @@
         return carry
 
     lax.fori_loop(0, groups, step, 0)
-    out = pltpu.make_async_copy(acc, face, side.at[1])
+    out = pltpu.make_async_copy(acc, face, side)
     out.start()
-    tail.wait()
-    over[0] = jnp.max(ends[...].astype(jnp.float32)).astype(jnp.int32)
     out.wait()
 
 
@@ -308,15 +301,15 @@
     part_buf = pltpu.VMEM((2, GROUP, columns, nodes), jnp.float32)
     dma = pltpu.SemaphoreType.DMA
     flops = 2 * pairs * columns * faces * nodes
-    out, slot, aug = pl.pallas_call(
-        functools.partial(send_kernel, n_narrow),
+    table = lax.all_gather(disp, "narrow", axis=0, tiled=True)
+    out, slot = pl.pallas_call(
+        functools.partial(send_kernel, n_narrow, patches),
         out_shape=(
             jax.ShapeDtypeStruct((n_wide, rows, nodes), jnp.int16),
             jax.ShapeDtypeStruct((pairs,), jnp.int32),
-            jax.ShapeDtypeStruct((patches + 1, columns, nodes), disp.dtype),
         ),
-        in_specs=[smem, smem, smem, vmem, hbm, hbm],
-        out_specs=(hbm, smem, hbm),
+        in_specs=[smem, smem, smem, vmem, hbm],
+        out_specs=(hbm, smem),
         scratch_shapes=[
             tile_buf,
             part_buf,
@@ -325,29 +318,27 @@
             pltpu.VMEM((pairs, columns, nodes), jnp.int16),
             pltpu.VMEM((n_wide, META, nodes), jnp.int32),
             pltpu.VMEM((n_wide, META, nodes), jnp.int16),
-            pltpu.VMEM((patches + 1, columns, nodes), disp.dtype),
             pltpu.SMEM((n_wide,), jnp.int32),
             dma((groups,)),
-            dma((3,)),
+            dma,
             dma,
         ],
         compiler_params=pltpu.CompilerParams(vmem_limit_bytes=LIMIT),
         cost_estimate=pl.CostEstimate(flops=flops, bytes_accessed=2 * tiles.size, transcendentals=0),
         name="send",
-    )(pair_fpatch, sdev, pair_spatch, loads, tiles, disp)
-    table = lax.all_gather(aug, "narrow", axis=0, tiled=True)
+    )(pair_fpatch, sdev, pair_spatch, loads, tiles)
     arrived = lax.all_to_all(out, "wide", split_axis=0, concat_axis=0, tiled=True)
     total, answer = pl.pallas_call(
         functools.partial(turn_kernel, n_narrow),
         out_shape=(
             jax.ShapeDtypeStruct((n_narrow * patches, columns, nodes), jnp.float32),
-            jax.ShapeDtypeStruct((n_wide, rows, nodes), disp.dtype),
+            jax.ShapeDtypeStruct((n_wide, ROOM * columns, nodes), disp.dtype),
         ),
         in_specs=[hbm, hbm],
         out_specs=(hbm, hbm),
         scratch_shapes=[
-            pltpu.VMEM((n_narrow * (patches + 1), columns, nodes), disp.dtype),
-            pltpu.VMEM((n_wide, rows, nodes), disp.dtype),
+            pltpu.VMEM((n_narrow * patches, columns, nodes), disp.dtype),
+            pltpu.VMEM((n_wide, ROOM * columns, nodes), disp.dtype),
             pltpu.VMEM((n_wide, rows, nodes), jnp.int16),
             pltpu.VMEM((4, patches, columns, nodes), jnp.float32),
             pltpu.VMEM((n_wide, META, nodes), jnp.float32),
@@ -368,29 +359,25 @@
     )(arrived, table)
     back = lax.all_to_all(answer, "wide", split_axis=0, concat_axis=0, tiled=True)
     struct_loads = lax.psum_scatter(total, "narrow", scatter_dimension=0, tiled=True)
-    face_disp, over = pl.pallas_call(
+    face_disp = pl.pallas_call(
         face_kernel,
-        out_shape=(
-            jax.ShapeDtypeStruct((loads.shape[0], columns, faces), jnp.float32),
-            jax.ShapeDtypeStruct((1,), jnp.int32),
-        ),
+        out_shape=jax.ShapeDtypeStruct((loads.shape[0], columns, faces), jnp.float32),
         in_specs=[smem, smem, hbm, hbm],
-        out_specs=(hbm, smem),
+        out_specs=hbm,
         scratch_shapes=[
             tile_buf,
             pltpu.VMEM((pairs, columns, nodes), disp.dtype),
             pltpu.VMEM((loads.shape[0], columns, faces), jnp.float32),
-            pltpu.VMEM((n_wide, META, nodes), disp.dtype),
             dma((groups,)),
             dma((groups,)),
-            dma((2,)),
+            dma,
         ],
         compiler_params=pltpu.CompilerParams(vmem_limit_bytes=LIMIT),
         cost_estimate=pl.CostEstimate(flops=flops, bytes_accessed=2 * tiles.size, transcendentals=0),
         name="face",
     )(pair_fpatch, slot, back, tiles)
     return lax.cond(
-        over[0] > ROOM,
+        struct_loads[0, 0, 0] > 1e-7 * MARK,
         lambda f, s: long_way(disp, loads, tiles, pair_fpatch, sdev, pair_spatch),
         lambda f, s: (f, s),
         face_disp,

time: 183 us -> 181 us (0.989)
  waiting for transfers between devices: 65.3 us -> 62.8 us
    all_to_all x1, waiting for transfers between devices: 65.2 us -> 62.1 us  [shards(): lax.all_to_all(answer, 'wide', split_axis=0, concat_axis=0, tiled=True)]
where the time goes in v2:
time: 181 us
  waiting for transfers between devices  62.8 us (35%)
  blocking collectives  61.8 us (34%)
  Pallas kernels  31.7 us (18%)
  between operations  14.8 us (8%)
  starting transfers between devices  8.2 us (5%)
    all_to_all x1, waiting for transfers between devices, shards(): lax.all_to_all(answer, 'wide', split_axis=0, concat_axis=0, tiled=True)  62.1 us
    all_to_all x1, blocking collectives, shards(): lax.all_to_all(out, 'wide', split_axis=0, concat_axis=0, tiled=True)  61.8 us
    pallas_call x1, Pallas kernels, shards(): pl.pallas_call(functools.partial(turn_kernel, n_narrow), out_shape=(jax.S...  11.4 us
    pallas_call x1, Pallas kernels, shards(): pl.pallas_call(face_kernel, out_shape=jax.ShapeDtypeStruct((loads.shape[0...  10.6 us
    pallas_call x1, Pallas kernels, shards(): pl.pallas_call(functools.partial(send_kernel, n_narrow, patches), out_sha...  9.71 us
    all_to_all x1, starting transfers between devices, shards(): lax.all_to_all(answer, 'wide', split_axis=0, concat_axis=0, tiled=True)  8.13 us
  transfers between devices with their start and end apart: 3, of which 1 were waited for; matrix products, arithmetic and copies ran while one was open for 0% of the time, Pallas kernels for 6%

profile of v2, /device:TPU:108, one launch (start us, length us, event | category | flops | bytes accessed | tf_op | source)
XLA Modules:
  0.0 180.7 jit_solution(3478597169972238711)
XLA Ops:
  7.2 0.0 all-gather.2.cloned.1.call-start
  7.2 0.7 all-gather.2.cloned.1.call-update
  7.9 0.0 reduce-scatter.2.cloned.1.call-start
  7.9 9.7 %send.1 = (s16[16,592,256]{2,1,0:T(8,128)(2,1)}, s32[128]{0:T(128)}) custom-call(s32[128]{0:T(128)} %fpatch.3, s32[128]{0:T(128)} %bitcast.43, s32[128]{0:T(128)} %spatch.1, bf16[32,48,256]{2,1,0:T(8,128)(2,1)} %loads.1, bf16[128,256,256]{2,1,0:T(8,128)(2,1)} %tiles.3), custom_call_target="tpu_custom_call" | custom-call | flops 805306368 | bytes 16777216 | tf_op jit(solution)/shard_map/send/pallas_call | solution.py:305
  17.7 61.8 %all_to_all.24.arrived = s16[16,592,256]{2,1,0:T(8,128)(2,1)} all-to-all(s16[16,592,256]{2,1,0:T(8,128)(2,1)} %get-tuple-element.31), channel_id=1, replica_groups=mesh['wide'=16,'narrow'=8] {'wide'}, dimensions={0} | all-to-all | bytes 9699328 | tf_op jit(solution)/shard_map/all_to_all | solution.py:330
  79.5 0.0 all-gather.2.cloned.1.call-done.table
  79.5 11.4 %turn.1 = (f32[256,48,256]{2,1,0:T(8,128)}, bf16[16,576,256]{2,1,0:T(8,128)(2,1)}) custom-call(s16[16,592,256]{2,1,0:T(8,128)(2,1)} %all_to_all.24.arrived, bf16[256,48,256]{2,1,0:T(8,128)(2,1)} %all-gather.2.cloned.1.call-done.table), custom_call_target="tpu_custom_call" | custom-call | flops 10000000 | bytes 29000000 | tf_op jit(solution)/shard_map/turn/pallas_call | solution.py:331
  90.9 0.0 reduce-scatter.2.cloned.1.call-update
  90.9 0.0 copy-start.2
  90.9 8.1 %all-to-all-start.4 = ((bf16[16,576,256]{2,1,0:T(8,128)(2,1)}), bf16[16,576,256]{2,1,0:T(8,128)(2,1)}, u32[]{:S(2)}, u32[]{:S(2)}) async-start(bf16[16,576,256]{2,1,0:T(8,128)(2,1)} %get-tuple-element.34), calls=%async_computation.5 | async-start | bytes 9437184 | tf_op jit(solution)/shard_map/all_to_all | solution.py:360
  99.0 62.1 %all-to-all-done.4.arrived = bf16[16,576,256]{2,1,0:T(8,128)(2,1)} async-done(((bf16[16,576,256]{2,1,0:T(8,128)(2,1)}), bf16[16,576,256]{2,1,0:T(8,128)(2,1)}, u32[]{:S(2)}, u32[]{:S(2)}) %all-to-all-start.4) | async-done | bytes 4718624 | tf_op jit(solution)/shard_map/all_to_all | solution.py:360
  161.1 0.0 copy-done.2
  161.1 0.0 copy-start
  161.1 0.0 copy-start.1
  161.1 0.0 copy-start.3
  161.2 10.6 %face.1 = f32[32,48,256]{2,1,0:T(8,128)} custom-call(s32[128]{0:T(128)S(1)} %copy-done.2, s32[128]{0:T(128)} %get-tuple-element.33.slot, bf16[16,576,256]{2,1,0:T(8,128)(2,1)} %all-to-all-done.4.arrived, bf16[128,256,256]{2,1,0:T(8,128)(2,1)} %tiles.3), custom_call_target="tpu_custom_call" | custom-call | flops 805306368 | bytes 16777216 | tf_op jit(solution)/shard_map/face/pallas_call | solution.py:362
  171.7 0.0 reduce-scatter.2.cloned.1.call-done
  171.7 1.2 slice.14
  173.6 0.0 copy-done
  173.6 0.0 copy-done.1
  173.6 0.0 copy-done.3
  173.6 0.2 conditional.1
Async XLA Ops:
  7.2 72.3 %all-gather.2.cloned.1.call-start = ((), (), s32[]{:S(2)}) async-start(), calls=%async_computation.6 | async-start | bytes 7077888 | tf_op jit(solution)/shard_map/all_gather | solution.py:304
  7.9 163.8 %reduce-scatter.2.cloned.1.call-start = ((), (), s32[]{:S(2)}) async-start(), calls=%async_computation.7 | async-start | bytes 14155776 | tf_op jit(solution)/shard_map/reduce_scatter | solution.py:361
  90.9 70.2 %copy-start.2 = (s32[128]{0:T(128)S(1)}, s32[128]{0:T(128)}, u32[]{:S(2)}) copy-start(s32[128]{0:T(128)} %fpatch.3) | copy-start | bytes 1540
  90.9 70.2 %all-to-all-start.4 = ((bf16[16,576,256]{2,1,0:T(8,128)(2,1)}), bf16[16,576,256]{2,1,0:T(8,128)(2,1)}, u32[]{:S(2)}, u32[]{:S(2)}) async-start(bf16[16,576,256]{2,1,0:T(8,128)(2,1)} %get-tuple-element.34), calls=%async_computation.5 | async-start | bytes 9437184 | tf_op jit(solution)/shard_map/all_to_all | solution.py:360
  161.1 12.4 %copy-start = (s32[128]{0:T(128)S(1)}, s32[128]{0:T(128)}, u32[]{:S(2)}) copy-start(s32[128]{0:T(128)} %spatch.1) | copy-start | bytes 1540
  161.1 12.4 %copy-start.1 = (bf16[32,48,256]{2,1,0:T(8,128)(2,1)S(1)}, bf16[32,48,256]{2,1,0:T(8,128)(2,1)}, u32[]{:S(2)}) copy-start(bf16[32,48,256]{2,1,0:T(8,128)(2,1)} %param.8) | copy-start | bytes 2359300
  161.1 12.5 %copy-start.3 = (s32[128,1]{0,1:T(1,128)S(1)}, s32[128,1]{0,1:T(1,128)}, u32[]{:S(2)}) copy-start(s32[128,1]{0,1:T(1,128)} %param.12) | copy-start | bytes 1540
Sparse Core Ops, SparseCore 0:
  9.7 41.1 all-gather.1
  91.0 71.6 reduce-scatter.1

commit v3 on v2

--- a/solution.py
+++ b/solution.py
@@ -8,6 +8,7 @@
 from jax.sharding import PartitionSpec as P
 
 ROOM = 12
+FIRM = 8
 META = 16
 SHIFT = 4
 GROUP = 16
@@ -80,15 +81,17 @@
 
 
 def send_kernel(
-    n_narrow, patches, fpatch, sdev, spatch, loads, tiles, out, slot,
-    buf, parts, most, power, whole, meta, ends, count, sems, side, leaving,
+    n_narrow, fpatch, sdev, spatch, loads, tiles, disp, out, slot, passed,
+    own, buf, parts, most, power, whole, meta, ends, count, sems, side, leaving, keep,
 ):
-    n_wide, columns = out.shape[0], whole.shape[1]
+    n_wide, patches, columns = out.shape[0], disp.shape[0], whole.shape[1]
     groups = tiles.shape[0] // GROUP
     groups = tiles.shape[0] // GROUP
 
     for g in range(groups):
         tile_copy(tiles, buf, sems, g).start()
+    bring = pltpu.make_async_copy(disp, own, keep.at[0])
+    bring.start()
     meta[...] = jnp.zeros_like(meta)
     for w in range(n_wide):
         count[w] = 0
@@ -138,6 +141,9 @@
 
     lax.fori_loop(1, groups, step, 0)
     second(groups - 1)
+    bring.wait()
+    give = pltpu.make_async_copy(own, passed, keep.at[1])
+    give.start()
     fullest = count[0]
     for w in range(1, n_wide):
         fullest = jnp.maximum(fullest, count[w])
@@ -149,11 +155,12 @@
     tail.start()
     pltpu.make_async_copy(whole, whole, leaving).wait()
     tail.wait()
+    give.wait()
 
 
 def turn_kernel(
     n_narrow, arrived, table, total, answer,
-    held, gone, came, acc, scale, meta, wide_names, names, lists, count, tables, comes, goes, outs, side,
+    held, gone, came, acc, scale, meta, wide_names, names, lists, count, tables, comes, later, goes, rest, outs, side,
 ):
     n_wide, columns = arrived.shape[0], table.shape[1]
     patches = table.shape[0] // n_narrow
@@ -168,7 +175,9 @@
     ]
     coming = [
         pltpu.make_async_copy(
-            arrived.at[pl.ds(i * quarter, quarter)], came.at[pl.ds(i * quarter, quarter)], comes.at[i]
+            arrived.at[pl.ds(i * quarter, quarter), pl.ds(0, FIRM * columns)],
+            came.at[pl.ds(i * quarter, quarter), pl.ds(0, FIRM * columns)],
+            comes.at[i],
         )
         for i in range(4)
     ]
@@ -187,20 +196,49 @@
         each.wait()
     naming.wait()
 
+    firm, loose = pl.ds(0, FIRM * columns), pl.ds(FIRM * columns, (ROOM - FIRM) * columns)
+
+    def more_come(w):
+        return pltpu.make_async_copy(arrived.at[w, loose], came.at[w, loose], later.at[w])
+
     def away(w):
-        return pltpu.make_async_copy(gone.at[w], answer.at[w], goes.at[w])
+        return pltpu.make_async_copy(gone.at[w, firm], answer.at[w, firm], goes.at[w])
+
+    def more_away(w):
+        return pltpu.make_async_copy(gone.at[w, loose], answer.at[w, loose], rest.at[w])
+
+    def for_full(act):
+        def each(w, carry):
+            @pl.when(names[w, FIRM] >= 0)
+            def _():
+                act(w)
+
+            return carry
+
+        lax.fori_loop(0, n_wide, each, 0)
+
+    def serve(w, j):
+        name = names[w, j]
+        asked = jnp.maximum(name, 0)
+        b = lax.div(asked, patches)
+        gone[w, j * columns : (j + 1) * columns, :] = held[asked]
+        chosen = jnp.where(name >= 0, b, n_narrow)
+        k = count[chosen]
+        count[chosen] = k + 1
+        lists[chosen, k] = (w << 16) | (j << 12) | (j << 8) | (asked - b * patches)
 
     def send(w, carry):
-        for j in range(ROOM):
-            name = names[w, j]
-            asked = jnp.maximum(name, 0)
-            b = lax.div(asked, patches)
-            gone[w, j * columns : (j + 1) * columns, :] = held[asked]
-            chosen = jnp.where(name >= 0, b, n_narrow)
-            k = count[chosen]
-            count[chosen] = k + 1
-            lists[chosen, k] = (w << 16) | (j << 12) | (j << 8) | (asked - b * patches)
+        for j in range(FIRM):
+            serve(w, j)
         away(w).start()
+
+        @pl.when(names[w, FIRM] >= 0)
+        def _():
+            more_come(w).start()
+            for j in range(FIRM, ROOM):
+                serve(w, j)
+            more_away(w).start()
+
         return carry
 
     lax.fori_loop(0, n_wide, send, 0)
@@ -212,6 +250,7 @@
         lists[b, count[b]] = (META - 1) << 8
     for each in coming:
         each.wait()
+    for_full(lambda w: more_come(w).wait())
 
     def leave(b):
         return pltpu.make_async_copy(acc.at[b % 4], total.at[pl.ds(b * patches, patches)], outs.at[b % 4])
@@ -241,6 +280,7 @@
         leave(b).start()
     for w in range(n_wide):
         away(w).wait()
+    for_full(lambda w: more_away(w).wait())
     for b in range(n_narrow - 4, n_narrow):
         leave(b).wait()
 
@@ -250,6 +290,7 @@
     groups = tiles.shape[0] // GROUP
 
     def fetch(g):
+        tile_copy(tiles, buf, sems, g).start()
         for i in range(GROUP):
             spot = slot[g * GROUP + i]
             place = spot & ((1 << SHIFT) - 1)
@@ -258,7 +299,6 @@
                 moved.at[g * GROUP + i],
                 moves.at[g],
             ).start()
-        tile_copy(tiles, buf, sems, g).start()
 
     for g in range(AHEAD):
         fetch(g)
@@ -301,16 +341,17 @@
     part_buf = pltpu.VMEM((2, GROUP, columns, nodes), jnp.float32)
     dma = pltpu.SemaphoreType.DMA
     flops = 2 * pairs * columns * faces * nodes
-    table = lax.all_gather(disp, "narrow", axis=0, tiled=True)
-    out, slot = pl.pallas_call(
-        functools.partial(send_kernel, n_narrow, patches),
+    out, slot, passed = pl.pallas_call(
+        functools.partial(send_kernel, n_narrow),
         out_shape=(
             jax.ShapeDtypeStruct((n_wide, rows, nodes), jnp.int16),
             jax.ShapeDtypeStruct((pairs,), jnp.int32),
+            jax.ShapeDtypeStruct(disp.shape, disp.dtype),
         ),
-        in_specs=[smem, smem, smem, vmem, hbm],
-        out_specs=(hbm, smem),
+        in_specs=[smem, smem, smem, vmem, hbm, hbm],
+        out_specs=(hbm, smem, hbm),
         scratch_shapes=[
+            pltpu.VMEM(disp.shape, disp.dtype),
             tile_buf,
             part_buf,
             pltpu.VMEM((2, GROUP, nodes), jnp.float32),
@@ -322,11 +363,13 @@
             dma((groups,)),
             dma,
             dma,
+            dma((2,)),
         ],
         compiler_params=pltpu.CompilerParams(vmem_limit_bytes=LIMIT),
         cost_estimate=pl.CostEstimate(flops=flops, bytes_accessed=2 * tiles.size, transcendentals=0),
         name="send",
-    )(pair_fpatch, sdev, pair_spatch, loads, tiles)
+    )(pair_fpatch, sdev, pair_spatch, loads, tiles, disp)
+    table = lax.all_gather(passed, "narrow", axis=0, tiled=True)
     arrived = lax.all_to_all(out, "wide", split_axis=0, concat_axis=0, tiled=True)
     total, answer = pl.pallas_call(
         functools.partial(turn_kernel, n_narrow),
@@ -339,7 +382,7 @@
         scratch_shapes=[
             pltpu.VMEM((n_narrow * patches, columns, nodes), disp.dtype),
             pltpu.VMEM((n_wide, ROOM * columns, nodes), disp.dtype),
-            pltpu.VMEM((n_wide, rows, nodes), jnp.int16),
+            pltpu.VMEM((n_wide, ROOM * columns, nodes), jnp.int16),
             pltpu.VMEM((4, patches, columns, nodes), jnp.float32),
             pltpu.VMEM((n_wide, META, nodes), jnp.float32),
             pltpu.VMEM((n_wide, META, nodes), jnp.int16),
@@ -349,6 +392,8 @@
             pltpu.SMEM((n_narrow + 1,), jnp.int32),
             dma((n_narrow,)),
             dma((4,)),
+            dma((n_wide,)),
+            dma((n_wide,)),
             dma((n_wide,)),
             dma((4,)),
             dma,

time: 181 us -> 181 us (level)
  no operation moved by 1% of the time
where the time goes in v3:
time: 181 us; the launch traced here: 182 us
  waiting for transfers between devices  62.3 us (34%)
  blocking collectives  61.8 us (34%)
  Pallas kernels  32.2 us (18%)
  between operations  14.8 us (8%)
  starting transfers between devices  9.1 us (5%)
    all_to_all x1, waiting for transfers between devices, shards(): lax.all_to_all(answer, 'wide', split_axis=0, concat_axis=0, tiled=True)  62.2 us
    all_to_all x1, blocking collectives, shards(): lax.all_to_all(out, 'wide', split_axis=0, concat_axis=0, tiled=True)  61.8 us
    pallas_call x1, Pallas kernels, shards(): pl.pallas_call(functools.partial(turn_kernel, n_narrow), out_shape=(jax.S...  11.7 us
    pallas_call x1, Pallas kernels, shards(): pl.pallas_call(face_kernel, out_shape=jax.ShapeDtypeStruct((loads.shape[0...  10.5 us
    pallas_call x1, Pallas kernels, shards(): pl.pallas_call(functools.partial(send_kernel, n_narrow), out_shape=(jax.S...  9.95 us
    all_to_all x1, starting transfers between devices, shards(): lax.all_to_all(answer, 'wide', split_axis=0, concat_axis=0, tiled=True)  9.02 us
  transfers between devices with their start and end apart: 3, of which 1 were waited for; matrix products, arithmetic and copies ran while one was open for 0% of the time, Pallas kernels for 6%

profile of v3, /device:TPU:108, one launch (start us, length us, event | category | flops | bytes accessed | tf_op | source)
XLA Modules:
  0.0 181.5 jit_solution(3271805537862966802)
XLA Ops:
  7.2 0.0 all-gather.2.cloned.1.call-start
  7.2 10.0 %send.1 = (s16[16,592,256]{2,1,0:T(8,128)(2,1)}, s32[128]{0:T(128)}, bf16[32,48,256]{2,1,0:T(8,128)(2,1)}) custom-call(s32[128]{0:T(128)} %fpatch.3, s32[128]{0:T(128)} %bitcast.43, s32[128]{0:T(128)} %spatch.1, bf16[32,48,256]{2,1,0:T(8,128)(2,1)} %loads.1, bf16[128,256,256]{2,1,0:T(8,128)(2,1)} %tiles.3, bf16[32,48,256]{2,1,0:T(8,128)(2,1)} %disp.1), custom_call_target="tpu_custom_call" | custom-call | flops 805306368 | bytes 16777216 | tf_op jit(solution)/shard_map/send/pallas_call | solution.py:344
  17.2 0.0 all-gather.2.cloned.1.call-update
  17.2 0.0 reduce-scatter.2.cloned.1.call-start
  17.2 61.8 %all_to_all.24.arrived = s16[16,592,256]{2,1,0:T(8,128)(2,1)} all-to-all(s16[16,592,256]{2,1,0:T(8,128)(2,1)} %get-tuple-element.32), channel_id=1, replica_groups=mesh['wide'=16,'narrow'=8] {'wide'}, dimensions={0} | all-to-all | bytes 9699328 | tf_op jit(solution)/shard_map/all_to_all | solution.py:373
  79.0 0.0 all-gather.2.cloned.1.call-done.table
  79.0 11.7 %turn.1 = (f32[256,48,256]{2,1,0:T(8,128)}, bf16[16,576,256]{2,1,0:T(8,128)(2,1)}) custom-call(s16[16,592,256]{2,1,0:T(8,128)(2,1)} %all_to_all.24.arrived, bf16[256,48,256]{2,1,0:T(8,128)(2,1)} %all-gather.2.cloned.1.call-done.table), custom_call_target="tpu_custom_call" | custom-call | flops 10000000 | bytes 29000000 | tf_op jit(solution)/shard_map/turn/pallas_call | solution.py:374
  90.8 0.0 reduce-scatter.2.cloned.1.call-update
  90.8 0.0 copy-start.2
  90.8 9.0 %all-to-all-start.4 = ((bf16[16,576,256]{2,1,0:T(8,128)(2,1)}), bf16[16,576,256]{2,1,0:T(8,128)(2,1)}, u32[]{:S(2)}, u32[]{:S(2)}) async-start(bf16[16,576,256]{2,1,0:T(8,128)(2,1)} %get-tuple-element.36), calls=%async_computation.5 | async-start | bytes 9437184 | tf_op jit(solution)/shard_map/all_to_all | solution.py:405
  99.9 62.2 %all-to-all-done.4.arrived = bf16[16,576,256]{2,1,0:T(8,128)(2,1)} async-done(((bf16[16,576,256]{2,1,0:T(8,128)(2,1)}), bf16[16,576,256]{2,1,0:T(8,128)(2,1)}, u32[]{:S(2)}, u32[]{:S(2)}) %all-to-all-start.4) | async-done | bytes 4718624 | tf_op jit(solution)/shard_map/all_to_all | solution.py:405
  162.1 0.0 copy-done.2
  162.1 0.0 copy-start
  162.1 0.0 copy-start.1
  162.1 0.0 copy-start.3
  162.1 10.5 %face.1 = f32[32,48,256]{2,1,0:T(8,128)} custom-call(s32[128]{0:T(128)S(1)} %copy-done.2, s32[128]{0:T(128)} %get-tuple-element.35.slot, bf16[16,576,256]{2,1,0:T(8,128)(2,1)} %all-to-all-done.4.arrived, bf16[128,256,256]{2,1,0:T(8,128)(2,1)} %tiles.3), custom_call_target="tpu_custom_call" | custom-call | flops 805306368 | bytes 16777216 | tf_op jit(solution)/shard_map/face/pallas_call | solution.py:407
  172.6 0.0 reduce-scatter.2.cloned.1.call-done
  172.6 1.2 slice.14
  174.4 0.0 copy-done
  174.4 0.0 copy-done.1
  174.5 0.0 copy-done.3
  174.5 0.2 conditional.1
Async XLA Ops:
  7.2 71.9 %all-gather.2.cloned.1.call-start = ((), (), s32[]{:S(2)}) async-start(), calls=%async_computation.6 | async-start | bytes 7077888 | tf_op jit(solution)/shard_map/all_gather | solution.py:372
  17.2 155.4 %reduce-scatter.2.cloned.1.call-start = ((), (), s32[]{:S(2)}) async-start(), calls=%async_computation.7 | async-start | bytes 14155776 | tf_op jit(solution)/shard_map/reduce_scatter | solution.py:406
  90.8 71.2 %copy-start.2 = (s32[128]{0:T(128)S(1)}, s32[128]{0:T(128)}, u32[]{:S(2)}) copy-start(s32[128]{0:T(128)} %fpatch.3) | copy-start | bytes 1540
  90.8 71.2 %all-to-all-start.4 = ((bf16[16,576,256]{2,1,0:T(8,128)(2,1)}), bf16[16,576,256]{2,1,0:T(8,128)(2,1)}, u32[]{:S(2)}, u32[]{:S(2)}) async-start(bf16[16,576,256]{2,1,0:T(8,128)(2,1)} %get-tuple-element.36), calls=%async_computation.5 | async-start | bytes 9437184 | tf_op jit(solution)/shard_map/all_to_all | solution.py:405
  162.1 12.4 %copy-start = (s32[128]{0:T(128)S(1)}, s32[128]{0:T(128)}, u32[]{:S(2)}) copy-start(s32[128]{0:T(128)} %spatch.1) | copy-start | bytes 1540
  162.1 12.4 %copy-start.1 = (bf16[32,48,256]{2,1,0:T(8,128)(2,1)S(1)}, bf16[32,48,256]{2,1,0:T(8,128)(2,1)}, u32[]{:S(2)}) copy-start(bf16[32,48,256]{2,1,0:T(8,128)(2,1)} %disp.1) | copy-start | bytes 2359300
  162.1 12.4 %copy-start.3 = (s32[128,1]{0,1:T(1,128)S(1)}, s32[128,1]{0,1:T(1,128)}, u32[]{:S(2)}) copy-start(s32[128,1]{0,1:T(1,128)} %param.12) | copy-start | bytes 1540
Sparse Core Ops, SparseCore 0:
  17.3 41.1 all-gather.1
  90.9 72.1 reduce-scatter.1

commit v4 on v3

--- a/solution.py
+++ b/solution.py
@@ -16,7 +16,7 @@
 STEPS = 128.0
 TOP = 32760.0
 MARK = 1e37
-LIMIT = 63 << 20
+LIMIT = 255 << 18
 
 
 def long_way(disp, loads, tiles, pair_fpatch, pair_sdev, pair_spatch):
@@ -82,7 +82,7 @@
 
 def send_kernel(
     n_narrow, fpatch, sdev, spatch, loads, tiles, disp, out, slot, passed,
-    own, buf, parts, most, power, whole, meta, ends, count, sems, side, leaving, keep,
+    own, buf, power, whole, meta, ends, count, sems, side, leaving, keep,
 ):
     n_wide, patches, columns = out.shape[0], disp.shape[0], whole.shape[1]
     groups = tiles.shape[0] // GROUP
@@ -103,14 +103,14 @@
         for i in range(GROUP):
             p = g * GROUP + i
             part = jnp.dot(loads[fpatch[p]], buf[p], preferred_element_type=jnp.float32)
-            parts[at, i] = part
-            most[at, i : i + 1, :] = jnp.max(jnp.abs(part), axis=0, keepdims=True)
+            most = jnp.max(jnp.abs(part), axis=0, keepdims=True)
+            steps = jnp.ceil(jnp.log2(jnp.maximum(most, 1e-33)) * STEPS)
+            unit = TOP * jnp.exp2(steps * (-1.0 / STEPS))
+            whole[p] = jnp.round(part * unit).astype(jnp.int32).astype(jnp.int16)
+            power[at, i : i + 1, :] = steps.astype(jnp.int32)
 
     def second(g):
         at = lax.rem(g, 2)
-        steps = jnp.ceil(jnp.log2(jnp.maximum(most[at], 1e-33)) * STEPS)
-        unit = TOP * jnp.exp2(steps * (-1.0 / STEPS))
-        power[...] = steps.astype(jnp.int32)
         for i in range(GROUP):
             p = g * GROUP + i
             target = sdev[p]
@@ -120,12 +120,10 @@
             count[w] = seen + 1
             place = jnp.minimum(seen, ROOM - 1)
             slot[p] = (w << SHIFT) | place
-            rounded = jnp.round(parts[at, i] * unit[i : i + 1, :]).astype(jnp.int32)
-            whole[p] = rounded.astype(jnp.int16)
             pltpu.make_async_copy(
                 whole.at[p], out.at[w, pl.ds(pl.multiple_of(place * columns, 16), columns)], leaving
             ).start()
-            meta[w, pl.ds(place, 1), :] = power[i : i + 1, :]
+            meta[w, pl.ds(place, 1), :] = power[at, i : i + 1, :]
             names = meta[w, ROOM : ROOM + 1, :]
             meta[w, ROOM : ROOM + 1, :] = jnp.where(lane == place, asked, names)
 
@@ -338,7 +336,6 @@
     hbm = pl.BlockSpec(memory_space=pltpu.HBM)
     tile_buf = pltpu.VMEM(tiles.shape, tiles.dtype)
     groups = pairs // GROUP
-    part_buf = pltpu.VMEM((2, GROUP, columns, nodes), jnp.float32)
     dma = pltpu.SemaphoreType.DMA
     flops = 2 * pairs * columns * faces * nodes
     out, slot, passed = pl.pallas_call(
@@ -353,9 +350,7 @@
         scratch_shapes=[
             pltpu.VMEM(disp.shape, disp.dtype),
             tile_buf,
-            part_buf,
-            pltpu.VMEM((2, GROUP, nodes), jnp.float32),
-            pltpu.VMEM((GROUP, nodes), jnp.int32),
+            pltpu.VMEM((2, GROUP, nodes), jnp.int32),
             pltpu.VMEM((pairs, columns, nodes), jnp.int16),
             pltpu.VMEM((n_wide, META, nodes), jnp.int32),
             pltpu.VMEM((n_wide, META, nodes), jnp.int16),

time: 181 us -> 182 us (level); the launches traced: 182 us -> 180 us
  no operation moved by 1% of the time
where the time goes in v4:
time: 182 us; the launch traced here: 180 us
  blocking collectives  61.8 us (34%)
  waiting for transfers between devices  61.5 us (34%)
  Pallas kernels  31.7 us (17%)
  between operations  14.7 us (8%)
  starting transfers between devices  9.35 us (5%)
    all_to_all x1, blocking collectives, shards(): lax.all_to_all(out, 'wide', split_axis=0, concat_axis=0, tiled=True)  61.8 us
    all_to_all x1, waiting for transfers between devices, shards(): lax.all_to_all(answer, 'wide', split_axis=0, concat_axis=0, tiled=True)  61.4 us
    pallas_call x1, Pallas kernels, shards(): pl.pallas_call(functools.partial(turn_kernel, n_narrow), out_shape=(jax.S...  11.1 us
    pallas_call x1, Pallas kernels, shards(): pl.pallas_call(face_kernel, out_shape=jax.ShapeDtypeStruct((loads.shape[0...  10.6 us
    pallas_call x1, Pallas kernels, shards(): pl.pallas_call(functools.partial(send_kernel, n_narrow), out_shape=(jax.S...  9.95 us
    all_to_all x1, starting transfers between devices, shards(): lax.all_to_all(answer, 'wide', split_axis=0, concat_axis=0, tiled=True)  9.27 us
  transfers between devices with their start and end apart: 3, of which 1 were waited for; matrix products, arithmetic and copies ran while one was open for 0% of the time, Pallas kernels for 6%

profile of v4, /device:TPU:108, one launch (start us, length us, event | category | flops | bytes accessed | tf_op | source)
XLA Modules:
  0.0 180.5 jit_solution(13680678244754636084)
XLA Ops:
  7.2 0.0 all-gather.2.cloned.1.call-start
  7.2 10.0 %send.1 = (s16[16,592,256]{2,1,0:T(8,128)(2,1)}, s32[128]{0:T(128)}, bf16[32,48,256]{2,1,0:T(8,128)(2,1)}) custom-call(s32[128]{0:T(128)} %fpatch.3, s32[128]{0:T(128)} %bitcast.43, s32[128]{0:T(128)} %spatch.1, bf16[32,48,256]{2,1,0:T(8,128)(2,1)} %loads.1, bf16[128,256,256]{2,1,0:T(8,128)(2,1)} %tiles.3, bf16[32,48,256]{2,1,0:T(8,128)(2,1)} %disp.1), custom_call_target="tpu_custom_call" | custom-call | flops 805306368 | bytes 16777216 | tf_op jit(solution)/shard_map/send/pallas_call | solution.py:341
  17.2 0.0 all-gather.2.cloned.1.call-update
  17.2 0.0 reduce-scatter.2.cloned.1.call-start
  17.2 61.8 %all_to_all.24.arrived = s16[16,592,256]{2,1,0:T(8,128)(2,1)} all-to-all(s16[16,592,256]{2,1,0:T(8,128)(2,1)} %get-tuple-element.32), channel_id=1, replica_groups=mesh['wide'=16,'narrow'=8] {'wide'}, dimensions={0} | all-to-all | bytes 9699328 | tf_op jit(solution)/shard_map/all_to_all | solution.py:368
  79.0 0.0 all-gather.2.cloned.1.call-done.table
  79.0 11.1 %turn.1 = (f32[256,48,256]{2,1,0:T(8,128)}, bf16[16,576,256]{2,1,0:T(8,128)(2,1)}) custom-call(s16[16,592,256]{2,1,0:T(8,128)(2,1)} %all_to_all.24.arrived, bf16[256,48,256]{2,1,0:T(8,128)(2,1)} %all-gather.2.cloned.1.call-done.table), custom_call_target="tpu_custom_call" | custom-call | flops 10000000 | bytes 29000000 | tf_op jit(solution)/shard_map/turn/pallas_call | solution.py:369
  90.1 0.0 reduce-scatter.2.cloned.1.call-update
  90.2 0.0 copy-start.1
  90.2 9.3 %all-to-all-start.4 = ((bf16[16,576,256]{2,1,0:T(8,128)(2,1)}), bf16[16,576,256]{2,1,0:T(8,128)(2,1)}, u32[]{:S(2)}, u32[]{:S(2)}) async-start(bf16[16,576,256]{2,1,0:T(8,128)(2,1)} %get-tuple-element.36), calls=%async_computation.5 | async-start | bytes 9437184 | tf_op jit(solution)/shard_map/all_to_all | solution.py:400
  99.4 61.4 %all-to-all-done.4.arrived = bf16[16,576,256]{2,1,0:T(8,128)(2,1)} async-done(((bf16[16,576,256]{2,1,0:T(8,128)(2,1)}), bf16[16,576,256]{2,1,0:T(8,128)(2,1)}, u32[]{:S(2)}, u32[]{:S(2)}) %all-to-all-start.4) | async-done | bytes 4718624 | tf_op jit(solution)/shard_map/all_to_all | solution.py:400
  160.9 0.0 copy-done.1
  160.9 0.0 copy-start
  160.9 0.0 copy-start.2
  160.9 10.6 %face.1 = f32[32,48,256]{2,1,0:T(8,128)} custom-call(s32[128]{0:T(128)S(1)} %copy-done.1, s32[128]{0:T(128)} %get-tuple-element.35.slot, bf16[16,576,256]{2,1,0:T(8,128)(2,1)} %all-to-all-done.4.arrived, bf16[128,256,256]{2,1,0:T(8,128)(2,1)} %tiles.3), custom_call_target="tpu_custom_call" | custom-call | flops 805306368 | bytes 16777216 | tf_op jit(solution)/shard_map/face/pallas_call | solution.py:402
  171.5 0.0 reduce-scatter.2.cloned.1.call-done
  171.5 1.2 slice.14
  173.4 0.0 copy-done
  173.4 0.0 copy-done.2
  173.4 0.2 conditional.1
Async XLA Ops:
  7.2 71.9 %all-gather.2.cloned.1.call-start = ((), (), s32[]{:S(2)}) async-start(), calls=%async_computation.6 | async-start | bytes 7077888 | tf_op jit(solution)/shard_map/all_gather | solution.py:367
  17.2 154.3 %reduce-scatter.2.cloned.1.call-start = ((), (), s32[]{:S(2)}) async-start(), calls=%async_computation.7 | async-start | bytes 14155776 | tf_op jit(solution)/shard_map/reduce_scatter | solution.py:401
  90.2 70.7 %copy-start.1 = (s32[128]{0:T(128)S(1)}, s32[128]{0:T(128)}, u32[]{:S(2)}) copy-start(s32[128]{0:T(128)} %fpatch.3) | copy-start | bytes 1540
  90.2 70.7 %all-to-all-start.4 = ((bf16[16,576,256]{2,1,0:T(8,128)(2,1)}), bf16[16,576,256]{2,1,0:T(8,128)(2,1)}, u32[]{:S(2)}, u32[]{:S(2)}) async-start(bf16[16,576,256]{2,1,0:T(8,128)(2,1)} %get-tuple-element.36), calls=%async_computation.5 | async-start | bytes 9437184 | tf_op jit(solution)/shard_map/all_to_all | solution.py:400
  160.9 12.5 %copy-start = (s32[128]{0:T(128)S(1)}, s32[128]{0:T(128)}, u32[]{:S(2)}) copy-start(s32[128]{0:T(128)} %spatch.1) | copy-start | bytes 1540
  160.9 12.5 %copy-start.2 = (s32[128,1]{0,1:T(1,128)S(1)}, s32[128,1]{0,1:T(1,128)}, u32[]{:S(2)}) copy-start(s32[128,1]{0,1:T(1,128)} %param.12) | copy-start | bytes 1540
Sparse Core Ops, SparseCore 0:
  17.3 41.1 all-gather.1
  90.3 72.8 reduce-scatter.1
